TPU v7x, 32 devices: a whole 2x2x4 slice. The times are simulated.
32 devices in a mesh: ctx: 16 (over z, y, core), tp: 2 (over x).
Axes of the slice: x: 2, y: 2, z: 4, core: 2. Of those that a mesh axis runs over, the one named last changes fastest.
Arguments:
- queries: bfloat16 [8192, 8192], P('ctx', 'tp'), may hold values from -8 to 8
- stacked_keys: bfloat16 [8192, 1024], P('ctx', 'tp'), may hold values from -8 to 8
- stacked_values: bfloat16 [8192, 1024], P('ctx', 'tp'), may hold values from -6 to 6
- doc_start: int32 [8192], P('ctx'), may hold values from 0 to 8191, as said below
- out_weight: bfloat16 [8192, 4096], P('tp'), may hold values from -0.0625 to 0.0625
Outputs:
- projected: bfloat16 [8192, 4096], P('ctx', 'tp')
Inputs may be any that keep to these rules, and one draw needn't show every extreme that they name: doc_start[t] is the position of the first token of the document holding token t; documents are contiguous runs of 1 to 4096 tokens, one document holds exactly 4096 tokens and does not begin at the first of a device's rows, and the last token forms a document of its own.
All inputs are finite; a program needn't handle non-finite values.
Results may differ from a plain program's by a relative error of at most 0.014.
Values may be sent and summed in bfloat16 or wider, within the bound.
No kernel may reach another device: no remote copies, remote signals or barrier semaphores. Data moves between devices by JAX's collectives and lax.ppermute only.
A program may use at most 128 MiB of HBM per device.

v0:
```python
import math

import jax
import jax.numpy as jnp
from jax import lax
from jax.sharding import PartitionSpec as P

HEAD_WIDTH = 128


masked_floor = -1e30


def shifted(block, axis, distance):
    devices = range(lax.axis_size(axis))
    route = [(i - distance, i) for i in devices if i - distance in devices]
    return lax.ppermute(block, axis, route)


def local(queries, stacked_keys, stacked_values, doc_start, out_weight):
    row_count = queries.shape[0]
    kv_local = stacked_keys.shape[1] // HEAD_WIDTH
    queries_per_group = queries.shape[1] // HEAD_WIDTH // kv_local
    score_scale = 1.0 / math.sqrt(HEAD_WIDTH)
    device_index = lax.axis_index("ctx")
    device_row = device_index * row_count
    grouped = queries.reshape(row_count, kv_local, queries_per_group, HEAD_WIDTH)
    query_pos = device_row + jnp.arange(row_count, dtype=jnp.int32)
    earliest = doc_start[0]
    latest = device_row + row_count - 1

    def attend(state, key_tile, value_tile, key_start):
        running_max, running_sum, accum = state
        count = key_tile.shape[0]
        key_heads = key_tile.reshape(count, kv_local, HEAD_WIDTH)
        value_heads = value_tile.reshape(count, kv_local, HEAD_WIDTH)
        scores = (
            jnp.einsum("qhgd,khd->hgqk", grouped, key_heads, preferred_element_type=jnp.float32)
            * score_scale
        )
        key_pos = key_start + jnp.arange(count, dtype=jnp.int32)
        visible = (key_pos[None, :] >= doc_start[:, None]) & (
            key_pos[None, :] <= query_pos[:, None]
        )
        scores = jnp.where(visible, scores, masked_floor)
        new_max = jnp.maximum(running_max, jnp.max(scores, axis=-1))
        rescale = jnp.exp(running_max - new_max)
        weights = jnp.where(visible, jnp.exp(scores - new_max[..., None]), 0.0)
        running_sum = running_sum * rescale + jnp.sum(weights, axis=-1)
        update = jnp.einsum(
            "hgqk,khd->hgqd",
            weights.astype(jnp.bfloat16),
            value_heads,
            preferred_element_type=jnp.float32,
        )
        accum = accum * rescale[..., None] + update
        return (new_max, running_sum, accum)

    def visit(state, key_tile, value_tile, key_start):
        count = key_tile.shape[0]
        needed = (key_start + count - 1 >= earliest) & (key_start <= latest)
        return lax.cond(
            needed,
            lambda inner: attend(inner, key_tile, value_tile, key_start),
            lambda inner: inner,
            state,
        )

    initial = (
        jnp.full((kv_local, queries_per_group, row_count), masked_floor, jnp.float32),
        jnp.zeros((kv_local, queries_per_group, row_count), jnp.float32),
        jnp.zeros((kv_local, queries_per_group, row_count, HEAD_WIDTH), jnp.float32),
    )
    state = attend(initial, stacked_keys, stacked_values, device_row)
    reach = lax.axis_size("ctx") // 2

    def relay_step(distance, carry):
        inner, key_tile, value_tile = carry
        key_tile, value_tile = shifted((key_tile, value_tile), "ctx", 1)
        inner = visit(inner, key_tile, value_tile, (device_index - distance) * row_count)
        return (inner, key_tile, value_tile)

    state, _, _ = lax.fori_loop(1, reach + 1, relay_step, (state, stacked_keys, stacked_values))
    _, running_sum, accum = state
    attended = (accum / running_sum[..., None]).astype(jnp.bfloat16)
    attended = attended.transpose(2, 0, 1, 3).reshape(
        row_count, kv_local * queries_per_group * HEAD_WIDTH
    )
    partial_value = jnp.dot(attended, out_weight, preferred_element_type=jnp.float32)
    return lax.psum_scatter(
        partial_value.astype(jnp.bfloat16), "tp", scatter_dimension=1, tiled=True
    )


def solution(mesh):
    return jax.shard_map(
        local,
        mesh=mesh,
        in_specs=(P("ctx", "tp"), P("ctx", "tp"), P("ctx", "tp"), P("ctx"), P("tp", None)),
        out_specs=P("ctx", "tp"),
        check_vma=False,
    )
```

profile of v0, /device:TPU:24, one launch (start us, length us, event | category | flops | bytes accessed | tf_op | source)
XLA Modules:
  0.0 706.4 jit_solution(11433785968611459705)
XLA Ops:
  10.9 6.4 copy.15
  17.4 6.2 copy.20
  23.6 16.0 %fusion.16 = (f32[4,8,512]{2,1,0:T(8,128)S(1)}, f32[4,512,512,8]{2,1,3,0:T(8,128)}) fusion(pred[512,512]{0,1:T(8,128)(4,1)S(1)} %compare_and_fusion.1, bf16[512,4,8,128]{0,3,2,1:T(8,128)(2,1)} %bitcast.41, bf16[512,4,128,1]{2,1,0,3:T(4,128)(2,1)S(1)} %bitcast.44), kind=kOutput, calls=%fused_computation.22 | convolution fusion | flops 2172633088 | bytes 38600704 | tf_op jit(solution)/shard_map/qhgd,khd->hgqk/dot_general | solution.py:38
  39.7 15.0 %fusion.18 = f32[4,8,512]{2,1,0:T(8,128)S(1)} fusion(f32[4,512,512,8]{2,1,3,0:T(8,128)} %get-tuple-element.519, f32[4,8,512]{2,1,0:T(8,128)S(1)} %broadcast_maximum_fusion, pred[512,512]{0,1:T(8,128)(4,1)S(1)} %compare_and_fusion.1), kind=kLoop, calls=%fused_computation.24 | loop fusion | flops 41926656 | bytes 33947648 | tf_op jit(solution)/shard_map/reduce_sum | solution.py:49
  54.9 18.1 %broadcast_add_fusion.1 = f32[4,8,512,128]{3,2,1,0:T(8,128)} fusion(f32[4,8,512]{2,1,0:T(8,128)S(1)} %get-tuple-element.516, f32[4,512,512,8]{2,1,3,0:T(8,128)} %get-tuple-element.519, f32[4,8,512]{2,1,0:T(8,128)S(1)} %broadcast_maximum_fusion, pred[512,512]{0,1:T(8,128)(4,1)S(1)} %compare_and_fusion.1, bf16[512,4,128,1]{2,1,0,3:T(4,128)(2,1)S(1)} %bitcast.45), kind=kOutput, calls=%fused_computation.29 | convolution fusion | flops 2191523840 | bytes 42860544 | tf_op jit(solution)/shard_map/hgqk,khd->hgqd/dot_general | solution.py:50
  73.0 420.2 %while.26 = (s32[]{:T(128)}, f32[4,8,512]{2,1,0:T(8,128)S(1)}, f32[4,8,512]{2,1,0:T(8,128)S(1)}, f32[4,8,512,128]{3,2,1,0:T(8,128)}, bf16[512,512]{1,0:T(8,128)(...) while((s32[]{:T(128)}, f32[4,8,512]{2,1,0:T(8,128)S(1)}, ...), condition=%wide.region_7.8_spmd.clone, body=%wide.region_2.7_spmd.clone.sunk | while | flops 4409033728 | bytes 133183912 | solution.py:83
  90.0 51.4 %conditional.3 = ((f32[4,8,512]{2,1,0:T(8,128)S(1)}, f32[4,8,512]{2,1,0:T(8,128)S(1)}, f32[4,8,512,128]{3,2,1,0:T(8,128)})) conditional(s32[]{:T(128)} %convert_element_type.40, (f32[4,8,512]{2,1,0:T(8,128)S(1)}, f32[4,8,512]{2,1,0:T(8,128)S(1)}, f32[4,8,512,128]{3,2,1,0:T(8,128)}) %tuple.64, (s32[]{:T(128)}, s32[512]{0:T(512)S(1)}, s32[]{:T(128)}, ...), branch_computations={%region_3.3_spmd, %region_4.6_spmd} | conditional | flops 4409033728 | bytes 126890024 | solution.py:62
  90.4 15.8 %fusion.2 = (f32[4,8,512]{2,1,0:T(8,128)S(1)}, f32[4,512,512,8]{2,1,3,0:T(8,128)}) fusion(pred[512,512]{0,1:T(8,128)(4,1)S(1)} %compare_and_fusion, bf16[512,4,8,128]{3,0,2,1:T(8,128)(2,1)} %get-tuple-element.417, bf16[512,4,128,1]{2,1,0,3:T(4,128)(2,1)S(1)} %bitcast.39), kind=kOutput, calls=%fused_computation.3 | convolution fusion | flops 2172633088 | bytes 38600704 | tf_op jit(solution)/shard_map/while/body/eval_jaxpr/cond/branch_1_fun/qhgd,khd->hgqk/dot_general | solution.py:38
  106.2 15.0 %fusion.4 = f32[4,8,512]{2,1,0:T(8,128)S(1)} fusion(f32[4,512,512,8]{2,1,3,0:T(8,128)} %get-tuple-element.513, f32[4,8,512]{2,1,0:T(8,128)S(1)} %max.2, pred[512,512]{0,1:T(8,128)(4,1)S(1)} %compare_and_fusion), kind=kLoop, calls=%fused_computation.5 | loop fusion | flops 41926656 | bytes 33947648 | tf_op jit(solution)/shard_map/while/body/eval_jaxpr/cond/branch_1_fun/reduce_sum | solution.py:49
  121.5 19.9 %multiply_add_fusion = f32[4,8,512,128]{3,2,1,0:T(8,128)} fusion(f32[4,8,512,128]{3,2,1,0:T(8,128)} %get-tuple-element.419, f32[4,8,512]{2,1,0:T(8,128)S(1)} %get-tuple-element.511, f32[4,512,512,8]{2,1,3,0:T(8,128)} %get-tuple-element.513, f32[4,8,512]{2,1,0:T(8,128)S(1)} %max.2, pred[512,512]{0,1:T(8,128)(4,1)S(1)} %compare_and_fusion, ...), kind=kOutput, calls=%fused_computation.8 | convolution fusion | flops 2193620992 | bytes 51249152 | tf_op jit(solution)/shard_map/while/body/eval_jaxpr/cond/branch_1_fun/hgqk,khd->hgqd/dot_general | solution.py:50
  146.7 6.1 collective-permute-done
  152.9 5.6 collective-permute-done.1
  158.5 51.4 %conditional.3 = ((f32[4,8,512]{2,1,0:T(8,128)S(1)}, f32[4,8,512]{2,1,0:T(8,128)S(1)}, f32[4,8,512,128]{3,2,1,0:T(8,128)})) conditional(s32[]{:T(128)} %convert_element_type.40, (f32[4,8,512]{2,1,0:T(8,128)S(1)}, f32[4,8,512]{2,1,0:T(8,128)S(1)}, f32[4,8,512,128]{3,2,1,0:T(8,128)}) %tuple.64, (s32[]{:T(128)}, s32[512]{0:T(512)S(1)}, s32[]{:T(128)}, ...), branch_computations={%region_3.3_spmd, %region_4.6_spmd} | conditional | flops 4409033728 | bytes 126890024 | solution.py:62
  158.9 15.8 %fusion.2 = (f32[4,8,512]{2,1,0:T(8,128)S(1)}, f32[4,512,512,8]{2,1,3,0:T(8,128)}) fusion(pred[512,512]{0,1:T(8,128)(4,1)S(1)} %compare_and_fusion, bf16[512,4,8,128]{3,0,2,1:T(8,128)(2,1)} %get-tuple-element.417, bf16[512,4,128,1]{2,1,0,3:T(4,128)(2,1)S(1)} %bitcast.39), kind=kOutput, calls=%fused_computation.3 | convolution fusion | flops 2172633088 | bytes 38600704 | tf_op jit(solution)/shard_map/while/body/eval_jaxpr/cond/branch_1_fun/qhgd,khd->hgqk/dot_general | solution.py:38
  174.7 15.0 %fusion.4 = f32[4,8,512]{2,1,0:T(8,128)S(1)} fusion(f32[4,512,512,8]{2,1,3,0:T(8,128)} %get-tuple-element.513, f32[4,8,512]{2,1,0:T(8,128)S(1)} %max.2, pred[512,512]{0,1:T(8,128)(4,1)S(1)} %compare_and_fusion), kind=kLoop, calls=%fused_computation.5 | loop fusion | flops 41926656 | bytes 33947648 | tf_op jit(solution)/shard_map/while/body/eval_jaxpr/cond/branch_1_fun/reduce_sum | solution.py:49
  190.0 19.9 %multiply_add_fusion = f32[4,8,512,128]{3,2,1,0:T(8,128)} fusion(f32[4,8,512,128]{3,2,1,0:T(8,128)} %get-tuple-element.419, f32[4,8,512]{2,1,0:T(8,128)S(1)} %get-tuple-element.511, f32[4,512,512,8]{2,1,3,0:T(8,128)} %get-tuple-element.513, f32[4,8,512]{2,1,0:T(8,128)S(1)} %max.2, pred[512,512]{0,1:T(8,128)(4,1)S(1)} %compare_and_fusion, ...), kind=kOutput, calls=%fused_computation.8 | convolution fusion | flops 2193620992 | bytes 51249152 | tf_op jit(solution)/shard_map/while/body/eval_jaxpr/cond/branch_1_fun/hgqk,khd->hgqd/dot_general | solution.py:50
  214.5 6.8 collective-permute-done
  227.0 51.4 %conditional.3 = ((f32[4,8,512]{2,1,0:T(8,128)S(1)}, f32[4,8,512]{2,1,0:T(8,128)S(1)}, f32[4,8,512,128]{3,2,1,0:T(8,128)})) conditional(s32[]{:T(128)} %convert_element_type.40, (f32[4,8,512]{2,1,0:T(8,128)S(1)}, f32[4,8,512]{2,1,0:T(8,128)S(1)}, f32[4,8,512,128]{3,2,1,0:T(8,128)}) %tuple.64, (s32[]{:T(128)}, s32[512]{0:T(512)S(1)}, s32[]{:T(128)}, ...), branch_computations={%region_3.3_spmd, %region_4.6_spmd} | conditional | flops 4409033728 | bytes 126890024 | solution.py:62
  227.4 15.8 %fusion.2 = (f32[4,8,512]{2,1,0:T(8,128)S(1)}, f32[4,512,512,8]{2,1,3,0:T(8,128)}) fusion(pred[512,512]{0,1:T(8,128)(4,1)S(1)} %compare_and_fusion, bf16[512,4,8,128]{3,0,2,1:T(8,128)(2,1)} %get-tuple-element.417, bf16[512,4,128,1]{2,1,0,3:T(4,128)(2,1)S(1)} %bitcast.39), kind=kOutput, calls=%fused_computation.3 | convolution fusion | flops 2172633088 | bytes 38600704 | tf_op jit(solution)/shard_map/while/body/eval_jaxpr/cond/branch_1_fun/qhgd,khd->hgqk/dot_general | solution.py:38
  243.2 15.0 %fusion.4 = f32[4,8,512]{2,1,0:T(8,128)S(1)} fusion(f32[4,512,512,8]{2,1,3,0:T(8,128)} %get-tuple-element.513, f32[4,8,512]{2,1,0:T(8,128)S(1)} %max.2, pred[512,512]{0,1:T(8,128)(4,1)S(1)} %compare_and_fusion), kind=kLoop, calls=%fused_computation.5 | loop fusion | flops 41926656 | bytes 33947648 | tf_op jit(solution)/shard_map/while/body/eval_jaxpr/cond/branch_1_fun/reduce_sum | solution.py:49
  258.5 19.9 %multiply_add_fusion = f32[4,8,512,128]{3,2,1,0:T(8,128)} fusion(f32[4,8,512,128]{3,2,1,0:T(8,128)} %get-tuple-element.419, f32[4,8,512]{2,1,0:T(8,128)S(1)} %get-tuple-element.511, f32[4,512,512,8]{2,1,3,0:T(8,128)} %get-tuple-element.513, f32[4,8,512]{2,1,0:T(8,128)S(1)} %max.2, pred[512,512]{0,1:T(8,128)(4,1)S(1)} %compare_and_fusion, ...), kind=kOutput, calls=%fused_computation.8 | convolution fusion | flops 2193620992 | bytes 51249152 | tf_op jit(solution)/shard_map/while/body/eval_jaxpr/cond/branch_1_fun/hgqk,khd->hgqd/dot_general | solution.py:50
  283.0 6.8 collective-permute-done
  295.6 48.8 %collective-permute-start = (bf16[512,512]{1,0:T(8,128)(2,1)S(1)}, bf16[512,512]{1,0:T(8,128)(2,1)S(1)}, u32[]{:S(2)}, u32[]{:S(2)}) collective-permute-start(bf16[512,512]{1,0:T(8,128)(2,1)S(1)} %get-tuple-element.624), channel_id=1, source_target_pairs={{0,2},{2,4},{4,6},{6,8},{8,10},{10,12},{12,14},{14,16},{16,18},{18... | collective-permute-start | bytes 1572872 | tf_op jit(solution)/shard_map/while/body/eval_jaxpr/ppermute | solution.py:17
  349.5 6.3 collective-permute-done.1
  360.6 55.7 %collective-permute-start.1 = (bf16[512,512]{1,0:T(8,128)(2,1)S(1)}, bf16[512,512]{1,0:T(8,128)(2,1)S(1)}, u32[]{:S(2)}, u32[]{:S(2)}) collective-permute-start(bf16[512,512]{1,0:T(8,128)(2,1)S(1)} %get-tuple-element.625), channel_id=1, source_target_pairs={{0,2},{2,4},{4,6},{6,8},{8,10},{10,12},{12,14},{14,16},{16,18},{18... | collective-permute-start | bytes 1572872 | tf_op jit(solution)/shard_map/while/body/eval_jaxpr/ppermute | solution.py:17
  418.0 10.2 %collective-permute-start = (bf16[512,512]{1,0:T(8,128)(2,1)S(1)}, bf16[512,512]{1,0:T(8,128)(2,1)S(1)}, u32[]{:S(2)}, u32[]{:S(2)}) collective-permute-start(bf16[512,512]{1,0:T(8,128)(2,1)S(1)} %get-tuple-element.624), channel_id=1, source_target_pairs={{0,2},{2,4},{4,6},{6,8},{8,10},{10,12},{12,14},{14,16},{16,18},{18... | collective-permute-start | bytes 1572872 | tf_op jit(solution)/shard_map/while/body/eval_jaxpr/ppermute | solution.py:17
  433.3 6.3 collective-permute-done.1
  439.7 42.0 %collective-permute-start = (bf16[512,512]{1,0:T(8,128)(2,1)S(1)}, bf16[512,512]{1,0:T(8,128)(2,1)S(1)}, u32[]{:S(2)}, u32[]{:S(2)}) collective-permute-start(bf16[512,512]{1,0:T(8,128)(2,1)S(1)} %get-tuple-element.624), channel_id=1, source_target_pairs={{0,2},{2,4},{4,6},{6,8},{8,10},{10,12},{12,14},{14,16},{16,18},{18... | collective-permute-start | bytes 1572872 | tf_op jit(solution)/shard_map/while/body/eval_jaxpr/ppermute | solution.py:17
  486.8 6.3 collective-permute-done.1
  493.2 8.7 %copy.21 = f32[4,8,512,128]{2,3,1,0:T(8,128)} copy(f32[4,8,512,128]{3,2,1,0:T(8,128)} %get-tuple-element.439) | data formatting | bytes 16777216 | tf_op jit(solution)/shard_map/while | solution.py:83
  506.6 23.4 %convolution_convert_fusion = bf16[512,4096]{1,0:T(8,128)(2,1)} fusion(bf16[512,4096]{0,1:T(8,128)(2,1)S(1)} %bitcast.43, bf16[4096,4096]{1,0:T(8,128)(2,1)} %param.13), kind=kOutput, calls=%fused_computation.28 | convolution fusion | flops 17181966336 | bytes 41943040 | tf_op jit(solution)/shard_map/dot_general | solution.py:89
  530.0 169.5 %reduce-scatter.2.cloned.1.call-done = bf16[512,2048]{1,0:T(8,128)(2,1)} async-done(((bf16[512,4096]{1,0:T(8,128)(2,1)}), bf16[512,2048]{1,0:T(8,128)(2,1)}) %reduce-scatter.2.cloned.1.call-update) | async-done | bytes 2097168 | tf_op jit(solution)/shard_map/reduce_scatter | solution.py:90
  (85 shorter events, 70.1 us)
Async XLA Ops:
  6.5 693.0 %reduce-scatter.2.cloned.1.call-start = ((), (), s32[]{:S(2)}) async-start(), calls=%async_computation.1 | async-start | bytes 6291456 | tf_op jit(solution)/shard_map/reduce_scatter | solution.py:90
  54.7 18.2 %copy-start = (s32[512]{0:T(512)S(1)}, s32[512]{0:T(512)}, u32[]{:S(2)}) copy-start(s32[512]{0:T(512)} %param.12) | copy-start | bytes 6148
  73.0 11.4 %collective-permute-start = (bf16[512,512]{1,0:T(8,128)(2,1)S(1)}, bf16[512,512]{1,0:T(8,128)(2,1)S(1)}, u32[]{:S(2)}, u32[]{:S(2)}) collective-permute-start(bf16[512,512]{1,0:T(8,128)(2,1)S(1)} %get-tuple-element.624), channel_id=1, source_target_pairs={{0,2},{2,4},{4,6},{6,8},{8,10},{10,12},{12,14},{14,16},{16,18},{18... | collective-permute-start | bytes 1572872 | tf_op jit(solution)/shard_map/while/body/eval_jaxpr/ppermute | solution.py:17
  74.9 15.1 %collective-permute-start.1 = (bf16[512,512]{1,0:T(8,128)(2,1)S(1)}, bf16[512,512]{1,0:T(8,128)(2,1)S(1)}, u32[]{:S(2)}, u32[]{:S(2)}) collective-permute-start(bf16[512,512]{1,0:T(8,128)(2,1)S(1)} %get-tuple-element.625), channel_id=1, source_target_pairs={{0,2},{2,4},{4,6},{6,8},{8,10},{10,12},{12,14},{14,16},{16,18},{18... | collective-permute-start | bytes 1572872 | tf_op jit(solution)/shard_map/while/body/eval_jaxpr/ppermute | solution.py:17
  141.5 11.4 %collective-permute-start = (bf16[512,512]{1,0:T(8,128)(2,1)S(1)}, bf16[512,512]{1,0:T(8,128)(2,1)S(1)}, u32[]{:S(2)}, u32[]{:S(2)}) collective-permute-start(bf16[512,512]{1,0:T(8,128)(2,1)S(1)} %get-tuple-element.624), channel_id=1, source_target_pairs={{0,2},{2,4},{4,6},{6,8},{8,10},{10,12},{12,14},{14,16},{16,18},{18... | collective-permute-start | bytes 1572872 | tf_op jit(solution)/shard_map/while/body/eval_jaxpr/ppermute | solution.py:17
  143.4 15.1 %collective-permute-start.1 = (bf16[512,512]{1,0:T(8,128)(2,1)S(1)}, bf16[512,512]{1,0:T(8,128)(2,1)S(1)}, u32[]{:S(2)}, u32[]{:S(2)}) collective-permute-start(bf16[512,512]{1,0:T(8,128)(2,1)S(1)} %get-tuple-element.625), channel_id=1, source_target_pairs={{0,2},{2,4},{4,6},{6,8},{8,10},{10,12},{12,14},{14,16},{16,18},{18... | collective-permute-start | bytes 1572872 | tf_op jit(solution)/shard_map/while/body/eval_jaxpr/ppermute | solution.py:17
  210.0 11.4 %collective-permute-start = (bf16[512,512]{1,0:T(8,128)(2,1)S(1)}, bf16[512,512]{1,0:T(8,128)(2,1)S(1)}, u32[]{:S(2)}, u32[]{:S(2)}) collective-permute-start(bf16[512,512]{1,0:T(8,128)(2,1)S(1)} %get-tuple-element.624), channel_id=1, source_target_pairs={{0,2},{2,4},{4,6},{6,8},{8,10},{10,12},{12,14},{14,16},{16,18},{18... | collective-permute-start | bytes 1572872 | tf_op jit(solution)/shard_map/while/body/eval_jaxpr/ppermute | solution.py:17
  211.9 15.1 %collective-permute-start.1 = (bf16[512,512]{1,0:T(8,128)(2,1)S(1)}, bf16[512,512]{1,0:T(8,128)(2,1)S(1)}, u32[]{:S(2)}, u32[]{:S(2)}) collective-permute-start(bf16[512,512]{1,0:T(8,128)(2,1)S(1)} %get-tuple-element.625), channel_id=1, source_target_pairs={{0,2},{2,4},{4,6},{6,8},{8,10},{10,12},{12,14},{14,16},{16,18},{18... | collective-permute-start | bytes 1572872 | tf_op jit(solution)/shard_map/while/body/eval_jaxpr/ppermute | solution.py:17
  278.4 11.4 %collective-permute-start = (bf16[512,512]{1,0:T(8,128)(2,1)S(1)}, bf16[512,512]{1,0:T(8,128)(2,1)S(1)}, u32[]{:S(2)}, u32[]{:S(2)}) collective-permute-start(bf16[512,512]{1,0:T(8,128)(2,1)S(1)} %get-tuple-element.624), channel_id=1, source_target_pairs={{0,2},{2,4},{4,6},{6,8},{8,10},{10,12},{12,14},{14,16},{16,18},{18... | collective-permute-start | bytes 1572872 | tf_op jit(solution)/shard_map/while/body/eval_jaxpr/ppermute | solution.py:17
  280.4 15.1 %collective-permute-start.1 = (bf16[512,512]{1,0:T(8,128)(2,1)S(1)}, bf16[512,512]{1,0:T(8,128)(2,1)S(1)}, u32[]{:S(2)}, u32[]{:S(2)}) collective-permute-start(bf16[512,512]{1,0:T(8,128)(2,1)S(1)} %get-tuple-element.625), channel_id=1, source_target_pairs={{0,2},{2,4},{4,6},{6,8},{8,10},{10,12},{12,14},{14,16},{16,18},{18... | collective-permute-start | bytes 1572872 | tf_op jit(solution)/shard_map/while/body/eval_jaxpr/ppermute | solution.py:17
  295.6 53.9 %collective-permute-start = (bf16[512,512]{1,0:T(8,128)(2,1)S(1)}, bf16[512,512]{1,0:T(8,128)(2,1)S(1)}, u32[]{:S(2)}, u32[]{:S(2)}) collective-permute-start(bf16[512,512]{1,0:T(8,128)(2,1)S(1)} %get-tuple-element.624), channel_id=1, source_target_pairs={{0,2},{2,4},{4,6},{6,8},{8,10},{10,12},{12,14},{14,16},{16,18},{18... | collective-permute-start | bytes 1572872 | tf_op jit(solution)/shard_map/while/body/eval_jaxpr/ppermute | solution.py:17
  344.4 11.4 %collective-permute-start.1 = (bf16[512,512]{1,0:T(8,128)(2,1)S(1)}, bf16[512,512]{1,0:T(8,128)(2,1)S(1)}, u32[]{:S(2)}, u32[]{:S(2)}) collective-permute-start(bf16[512,512]{1,0:T(8,128)(2,1)S(1)} %get-tuple-element.625), channel_id=1, source_target_pairs={{0,2},{2,4},{4,6},{6,8},{8,10},{10,12},{12,14},{14,16},{16,18},{18... | collective-permute-start | bytes 1572872 | tf_op jit(solution)/shard_map/while/body/eval_jaxpr/ppermute | solution.py:17
  355.9 61.2 %collective-permute-start = (bf16[512,512]{1,0:T(8,128)(2,1)S(1)}, bf16[512,512]{1,0:T(8,128)(2,1)S(1)}, u32[]{:S(2)}, u32[]{:S(2)}) collective-permute-start(bf16[512,512]{1,0:T(8,128)(2,1)S(1)} %get-tuple-element.624), channel_id=1, source_target_pairs={{0,2},{2,4},{4,6},{6,8},{8,10},{10,12},{12,14},{14,16},{16,18},{18... | collective-permute-start | bytes 1572872 | tf_op jit(solution)/shard_map/while/body/eval_jaxpr/ppermute | solution.py:17
  360.6 57.3 %collective-permute-start.1 = (bf16[512,512]{1,0:T(8,128)(2,1)S(1)}, bf16[512,512]{1,0:T(8,128)(2,1)S(1)}, u32[]{:S(2)}, u32[]{:S(2)}) collective-permute-start(bf16[512,512]{1,0:T(8,128)(2,1)S(1)} %get-tuple-element.625), channel_id=1, source_target_pairs={{0,2},{2,4},{4,6},{6,8},{8,10},{10,12},{12,14},{14,16},{16,18},{18... | collective-permute-start | bytes 1572872 | tf_op jit(solution)/shard_map/while/body/eval_jaxpr/ppermute | solution.py:17
  418.0 15.3 %collective-permute-start = (bf16[512,512]{1,0:T(8,128)(2,1)S(1)}, bf16[512,512]{1,0:T(8,128)(2,1)S(1)}, u32[]{:S(2)}, u32[]{:S(2)}) collective-permute-start(bf16[512,512]{1,0:T(8,128)(2,1)S(1)} %get-tuple-element.624), channel_id=1, source_target_pairs={{0,2},{2,4},{4,6},{6,8},{8,10},{10,12},{12,14},{14,16},{16,18},{18... | collective-permute-start | bytes 1572872 | tf_op jit(solution)/shard_map/while/body/eval_jaxpr/ppermute | solution.py:17
  428.2 11.4 %collective-permute-start.1 = (bf16[512,512]{1,0:T(8,128)(2,1)S(1)}, bf16[512,512]{1,0:T(8,128)(2,1)S(1)}, u32[]{:S(2)}, u32[]{:S(2)}) collective-permute-start(bf16[512,512]{1,0:T(8,128)(2,1)S(1)} %get-tuple-element.625), channel_id=1, source_target_pairs={{0,2},{2,4},{4,6},{6,8},{8,10},{10,12},{12,14},{14,16},{16,18},{18... | collective-permute-start | bytes 1572872 | tf_op jit(solution)/shard_map/while/body/eval_jaxpr/ppermute | solution.py:17
  439.7 47.1 %collective-permute-start = (bf16[512,512]{1,0:T(8,128)(2,1)S(1)}, bf16[512,512]{1,0:T(8,128)(2,1)S(1)}, u32[]{:S(2)}, u32[]{:S(2)}) collective-permute-start(bf16[512,512]{1,0:T(8,128)(2,1)S(1)} %get-tuple-element.624), channel_id=1, source_target_pairs={{0,2},{2,4},{4,6},{6,8},{8,10},{10,12},{12,14},{14,16},{16,18},{18... | collective-permute-start | bytes 1572872 | tf_op jit(solution)/shard_map/while/body/eval_jaxpr/ppermute | solution.py:17
  481.7 11.4 %collective-permute-start.1 = (bf16[512,512]{1,0:T(8,128)(2,1)S(1)}, bf16[512,512]{1,0:T(8,128)(2,1)S(1)}, u32[]{:S(2)}, u32[]{:S(2)}) collective-permute-start(bf16[512,512]{1,0:T(8,128)(2,1)S(1)} %get-tuple-element.625), channel_id=1, source_target_pairs={{0,2},{2,4},{4,6},{6,8},{8,10},{10,12},{12,14},{14,16},{16,18},{18... | collective-permute-start | bytes 1572872 | tf_op jit(solution)/shard_map/while/body/eval_jaxpr/ppermute | solution.py:17
Sparse Core Ops, SparseCore 0:
  530.2 169.3 reduce-scatter.1
where the time goes:
time: 714 us; the launch traced here: 706 us
  waiting for transfers between devices  237 us (33%)
  starting transfers between devices  192 us (27%)
  matrix products  165 us (23%)
  other arithmetic  66.8 us (9%)
  local copies, waits for them, and re-layouts  26.3 us (4%)
  between operations  13.5 us (2%)
    ppermute x16, starting transfers between devices, shifted(): return lax.ppermute(block, axis, route)  192 us
    reduce_scatter x1, waiting for transfers between devices, local(): lax.psum_scatter(partial_value.astype(jnp.bfloat16), 'tp', scatter_dimens...  170 us
    dot_general x4, matrix products, attend(): jnp.einsum('hgqk,khd->hgqd', weights.astype(jnp.bfloat16), value_heads, p...  77.8 us
    ppermute x16, waiting for transfers between devices, shifted(): return lax.ppermute(block, axis, route)  67.1 us
    dot_general x4, matrix products, attend(): jnp.einsum('qhgd,khd->hgqk', grouped, key_heads, preferred_element_type=j...  63.5 us
    reduce_sum x4, other arithmetic, attend(): running_sum = running_sum * rescale + jnp.sum(weights, axis=-1)  60.1 us
    dot_general x1, matrix products, local(): jnp.dot(attended, out_weight, preferred_element_type=jnp.float32)  23.4 us
    unnamed x6, local copies, waits for them, and re-layouts  14.7 us
  transfers between devices with their start and end apart: 17, of which 13 were waited for; matrix products, arithmetic and copies ran while one was open for 0% of the time, Pallas kernels for 0%

commit v1 on v0

v1 whole, which is shorter than its diff:
```python
import functools
import math

import jax
import jax.numpy as jnp
from jax import lax
from jax.experimental import pallas as pl
from jax.experimental.pallas import tpu as pltpu
from jax.sharding import PartitionSpec as P

D = 128
GROUP = 8
WIDTH = GROUP * D
UNIT = 512
SCALE = math.log2(math.e) / math.sqrt(D)
SAFE = 4800.0
FLOOR = -1e30
NT = (((1,), (1,)), ((), ()))
F32 = jnp.float32
BF16 = jnp.bfloat16


def params(mib=40):
    return pltpu.CompilerParams(vmem_limit_bytes=mib * 2**20)


def pack_body(me_ref, *refs):
    count = len(refs) // 3
    for i in range(count):
        k_ref, v_ref, out_ref = refs[2 * i], refs[2 * i + 1], refs[2 * count + i]
        out_ref[0, 0] = k_ref[...]
        for j in range(k_ref.shape[0] // D):
            out_ref[0, 1, j * D : (j + 1) * D, :] = v_ref[j * D : (j + 1) * D, :].T


def pack(me, keys, values, held, split):
    rows = keys.shape[0]
    picks = [lambda g, me: (0, g + lax.rem(me[0], 2) * held if split else g)]
    if split:
        picks.append(lambda g, me: (0, g + (1 - lax.rem(me[0], 2)) * held))
    return pl.pallas_call(
        pack_body,
        grid_spec=pltpu.PrefetchScalarGridSpec(
            num_scalar_prefetch=1,
            grid=(held,),
            in_specs=[pl.BlockSpec((rows, D), pick) for pick in picks for _ in range(2)],
            out_specs=[pl.BlockSpec((1, 2, rows, D), lambda g, me: (g, 0, 0, 0))] * len(picks),
        ),
        out_shape=[jax.ShapeDtypeStruct((held, 2, rows, D), BF16)] * len(picks),
        compiler_params=params(),
        name="pack",
    )(me, *[keys, values] * len(picks))


def largest_norm(x):
    squares = (x.astype(F32) * x.astype(F32)).astype(BF16)
    return jnp.max(jnp.dot(squares, jnp.ones((D, D), BF16), preferred_element_type=F32))


def norms_body(me_ref, *refs):
    for side, q_ref in enumerate(refs[:-1]):
        largest = largest_norm(q_ref[:, :D])
        for h in range(1, GROUP):
            largest = jnp.maximum(largest, largest_norm(q_ref[:, h * D : (h + 1) * D]))
        refs[-1][pl.program_id(0) * (len(refs) - 1) + side] = largest


def norms(me, queries, first_head, held):
    rows = queries[0].shape[0]
    return pl.pallas_call(
        norms_body,
        grid_spec=pltpu.PrefetchScalarGridSpec(
            num_scalar_prefetch=1,
            grid=(held,),
            in_specs=[pl.BlockSpec((rows, WIDTH), lambda h, me: (0, first_head(me) + h))]
            * len(queries),
            out_specs=pl.BlockSpec(memory_space=pltpu.SMEM),
        ),
        out_shape=jax.ShapeDtypeStruct((held * len(queries),), F32),
        compiler_params=params(),
        name="norms",
    )(me, *queries)


def attend_body(
    me_ref, *refs, head, slots, sides, group, rows, tile, row, distance, first, last
):
    doc_values, refs = refs[:sides], refs[sides:]
    kv, refs = refs[:slots], refs[slots:]
    docs, refs = refs[:sides], refs[sides:]
    q_refs, q_norms, refs = refs[: len(group)], refs[len(group)], refs[len(group) + 1 :]
    if not first:
        old_acc, old_stat, old_flag, refs = refs[0], refs[1], refs[2], refs[3:]
    if last:
        outs, refs = refs[: len(group)], refs[len(group) :]
        acc, stat, refs = refs[0], refs[1], refs[2:]
    else:
        acc, stat, new_flag, refs = refs[0].at[0], refs[1].at[0], refs[2], refs[3:]
    keys, values, peak, mask, norm, held_q = refs
    me = me_ref[0]
    core = lax.rem(me, 2)
    chip = lax.div(me, 2)
    span = 2 * rows
    stack = UNIT // tile
    units = GROUP // stack
    side = group[0] + pl.program_id(0)

    @pl.when(pl.program_id(0) == 0)
    def _():
        largest = jnp.float32(0)
        for s in range(slots):
            block = kv[s][0].reshape(span, D)
            keys[s * span : (s + 1) * span, :] = block
            largest = jnp.maximum(largest, largest_norm(block))
            for b in range(2):
                for j in range(0, rows, D):
                    at = s * span + b * rows + j
                    values[:, at : at + D] = kv[s][1, b, j : j + D, :]
        norm[0] = largest

    if len(group) == 1:
        q_ref = q_refs[0]
    else:
        q_ref = held_q
        for k in range(len(group)):

            @pl.when(side == group[k])
            def _():
                q_ref[...] = q_refs[k][...]

    def of_side(pieces):
        return pieces[0] if sides == 1 else jnp.where(side == 0, pieces[0], pieces[1])

    part = jnp.where(side == 0, core, 1 - core)
    top = (2 * chip + part) * rows + row
    lowest = of_side([doc[row] for doc in doc_values])
    highest = of_side([doc[row + tile - 1] for doc in doc_values])
    begin = of_side([doc[...] for doc in docs])
    begin = jnp.concatenate([begin] * stack, axis=1)
    place = lax.broadcasted_iota(jnp.int32, (1, UNIT), 1)
    place = top + (lax.rem(place, tile) if stack > 1 else place)

    if first:
        acc[...] = jnp.zeros_like(acc)
        stat[...] = jnp.zeros_like(stat)
    else:
        acc[...] = old_acc[0]
        stat[...] = old_stat[0]
    plain = norm[0] * q_norms[head * sides + side] / D <= SAFE
    if not first:
        plain = plain & (old_flag[side] == 0)
    if not last:
        new_flag[side] = jnp.where(plain, 0, 1)

    def attend_side(q_ref):
        def scores(at, count, u):
            block = keys[pl.ds(at, count), :]
            q = [q_ref[:, pl.ds((u * stack + i) * D, D)] for i in range(stack)]
            q = q[0] if stack == 1 else jnp.concatenate(q, axis=0)
            return lax.dot_general(block, q, NT, preferred_element_type=F32)

        def add(at, count, u, weights):
            stat[u, :8] += jnp.sum(weights.reshape(count // 8, 8, UNIT), axis=0)
            block = values[:, pl.ds(at, count)]
            acc[u] += jnp.dot(block, weights.astype(BF16), preferred_element_type=F32)

        def run(at, count, masked):
            now = scores(at, count, 0)
            for u in range(units):
                later = scores(at, count, u + 1) if u + 1 < units else None
                weights = jnp.exp2(now * SCALE)
                if masked:
                    weights = weights * mask[...]
                add(at, count, u, weights)
                now = later

        def run_shifted(at):
            def unit(u, _):
                visible = mask[...] > 0.0
                now = jnp.where(visible, scores(at, rows, u) * SCALE, FLOOR)
                old = peak[u]
                new = jnp.maximum(old, jnp.max(now, axis=0, keepdims=True))
                fade = jnp.exp2(old - new)
                peak[u] = new
                stat[u, :8] = stat[u, :8] * fade
                acc[u] = acc[u] * fade
                add(at, rows, u, jnp.where(visible, jnp.exp2(now - new), 0.0))
                return 0

            lax.fori_loop(0, units, unit, 0)

        def start_of(s):
            far = jnp.int32(distance(0, me))
            for k in range(1, slots):
                far = jnp.where(s == k, distance(k, me), far)
            return (chip - far) * span

        def is_whole(start):
            return (start >= highest) & (start + span <= top + 1)

        def edges(skip_whole, body):
            def block(n, _):
                start = start_of(lax.div(n, 2))
                key_start = start + jnp.where(lax.rem(n, 2) == 0, core, 1 - core) * rows
                needed = (key_start + rows > lowest) & (key_start < top + tile)
                if skip_whole:
                    needed = needed & jnp.logical_not(is_whole(start))

                @pl.when(needed)
                def _():
                    position = key_start + lax.broadcasted_iota(jnp.int32, (rows, UNIT), 0)
                    mask[...] = ((position >= begin) & (position <= place)).astype(F32)
                    body(pl.multiple_of(n * rows, rows))

                return 0

            lax.fori_loop(0, 2 * slots, block, 0)

        @pl.when(plain)
        def _():
            def whole_slot(s, _):
                @pl.when(is_whole(start_of(s)))
                def _():
                    run(pl.multiple_of(s * span, span), span, False)

                return 0

            lax.fori_loop(0, slots, whole_slot, 0)
            edges(True, lambda at: run(at, rows, True))

        @pl.when(jnp.logical_not(plain))
        def _():
            for u in range(units):
                some = jnp.sum(stat[u, :8], axis=0, keepdims=True) > 0.0
                peak[u] = jnp.where(some, stat[u, 8:9], FLOOR)
            edges(False, run_shifted)
            for u in range(units):
                stat[u, 8:] = jnp.broadcast_to(peak[u], (8, UNIT))

    attend_side(q_ref)

    if last:
        for k in range(len(group)):

            @pl.when(side == group[k])
            def _():
                for u in range(units):
                    inverse = 1.0 / jnp.sum(stat[u, :8], axis=0, keepdims=True)
                    mean = (acc[u] * inverse).astype(BF16).T
                    for i in range(stack):
                        h = u * stack + i
                        outs[k][:, h * D : (h + 1) * D] = mean[i * tile : (i + 1) * tile]


def attend(me, doc_values, kv, distance, docs, queries, first_head, q_norms, head, group, state, last, tile, row):
    slots, sides = len(kv), len(docs)
    rows = docs[0].shape[1]
    first = state is None
    units = GROUP * tile // UNIT
    acc_shape = (units, D, UNIT)
    stat_shape = (units, 16, UNIT)
    in_smem = pl.BlockSpec(memory_space=pltpu.SMEM)
    state_specs = [
        pl.BlockSpec((1,) + shape, lambda i, *s: (group[0] + i, 0, 0, 0)) for shape in (acc_shape, stat_shape)
    ] + [in_smem]
    if last:
        out_specs = [pl.BlockSpec((tile, WIDTH), lambda i, *s: (0, 0))] * len(group)
        out_shape = [jax.ShapeDtypeStruct((tile, WIDTH), BF16)] * len(group)
        held = [pltpu.VMEM(acc_shape, F32), pltpu.VMEM(stat_shape, F32)]
    else:
        out_specs = state_specs
        out_shape = [
            jax.ShapeDtypeStruct((sides,) + shape, F32) for shape in (acc_shape, stat_shape)
        ] + [jax.ShapeDtypeStruct((sides,), jnp.int32)]
        held = []
    work = len(group) * GROUP * tile * slots * 2 * rows
    return pl.pallas_call(
        functools.partial(
            attend_body,
            head=head,
            slots=slots,
            sides=sides,
            group=group,
            rows=rows,
            tile=tile,
            row=row,
            distance=distance,
            first=first,
            last=last,
        ),
        grid_spec=pltpu.PrefetchScalarGridSpec(
            num_scalar_prefetch=1 + sides,
            grid=(len(group),),
            in_specs=[pl.BlockSpec(kv[0].shape, lambda i, *s: (0, 0, 0, 0))] * slots
            + [pl.BlockSpec((1, tile), lambda i, *s: (0, row // tile))] * sides
            + [pl.BlockSpec((tile, WIDTH), lambda i, *s: (row // tile, first_head(s[0]) + head))]
            * len(group)
            + [in_smem]
            + ([] if first else state_specs),
            out_specs=out_specs,
            scratch_shapes=held
            + [
                pltpu.VMEM((slots * 2 * rows, D), BF16),
                pltpu.VMEM((D, slots * 2 * rows), BF16),
                pltpu.VMEM((units, 1, UNIT), F32),
                pltpu.VMEM((rows, UNIT), F32),
                pltpu.SMEM((1,), F32),
                pltpu.VMEM((tile, WIDTH), BF16),
            ],
        ),
        out_shape=out_shape,
        compiler_params=params(),
        cost_estimate=pl.CostEstimate(
            flops=work * D * 6, bytes_accessed=8 * 2**20, transcendentals=work
        ),
        name="attend",
    )(me, *doc_values, *kv, *docs, *[queries[k] for k in group], q_norms, *([] if first else state))


def project_body(me_ref, *refs, blocks):
    count = len(blocks)
    w_ref, out_ref = refs[count], refs[count + 1]
    total = None
    for a, block in zip(refs[:count], blocks):
        at = pl.multiple_of(block(me_ref) * WIDTH, WIDTH)
        term = jnp.dot(a[...], w_ref[pl.ds(at, WIDTH), :], preferred_element_type=F32)
        total = term if total is None else total + term
    out_ref[...] = total.astype(BF16)


def project(me, parts, rows, weight, column, cols):
    tile = min(cols, 256)
    depth = weight.shape[0]
    return pl.pallas_call(
        functools.partial(project_body, blocks=[block for _, _, block in parts]),
        grid_spec=pltpu.PrefetchScalarGridSpec(
            num_scalar_prefetch=1,
            grid=(cols // tile,),
            in_specs=[
                pl.BlockSpec((rows, WIDTH), lambda n, me, at=at: (at, 0)) for _, at, _ in parts
            ]
            + [pl.BlockSpec((depth, tile), lambda n, me: (0, column(me) // tile + n))],
            out_specs=pl.BlockSpec((rows, tile), lambda n, me: (0, n)),
        ),
        out_shape=jax.ShapeDtypeStruct((rows, cols), BF16),
        compiler_params=params(32),
        cost_estimate=pl.CostEstimate(
            flops=2 * rows * cols * depth, bytes_accessed=2 * cols * depth, transcendentals=0
        ),
        name="project",
    )(me, *[a for a, _, _ in parts], weight)


def local(queries, stacked_keys, stacked_values, doc_start, out_weight):
    rows = queries.shape[0]
    heads = stacked_keys.shape[1] // D
    ctx = lax.axis_size("ctx")
    tp = lax.axis_size("tp")
    levels = ctx // 2 // 4
    index = lax.axis_index("ctx")
    me = jnp.stack([index, lax.axis_index("tp")]).astype(jnp.int32)
    is_y0 = lax.rem(lax.div(index, 2), 2) == 0
    split = heads % 2 == 0
    held = heads // 2 if split else heads

    def permuted(x, target):
        return lax.ppermute(x, "ctx", [(i, target(i)) for i in range(ctx)])

    def other_core(x):
        return permuted(x, lambda i: i ^ 1)

    def other_y(x):
        return permuted(x, lambda i: i ^ 2)

    def next_z(x):
        return permuted(x, lambda i: (i + 4) % ctx)

    def after(x, *others):
        return lax.optimization_barrier((x,) + others)[0]

    packed = pack(me, stacked_keys, stacked_values, held, split)
    mine = packed[0]
    theirs = other_core(packed[-1])
    doc_values, docs = [doc_start], [doc_start.reshape(1, rows)]
    owns = [jnp.stack([mine[h], theirs[h]], axis=1) for h in range(held)]
    queries = [queries]

    def first_head(me):
        return lax.rem(me[0], 2) * held if split else 0

    if split:
        doc_values.append(other_core(after(doc_start, owns[0])))
        docs.append(doc_values[1].reshape(1, rows))
        queries.append(other_core(after(queries[0], owns[0])))
    q_norms = norms(me, queries, first_head, held)

    def along_distance(level):
        return lambda me: 2 * level

    def across_distance(level):
        if level < levels:
            return lambda me: 2 * level + 2 * lax.rem(lax.div(me, 2), 2) - 1
        return lambda me: jnp.where(lax.rem(lax.div(me, 2), 2) == 0, 2 * levels - 1, 1)

    sides = tuple(range(len(docs)))

    def call(slots, head, group, state, last, tile=rows, row=0):
        return attend(
            me,
            doc_values,
            [x for x, _ in slots],
            lambda s, me: slots[s][1](me),
            docs,
            queries,
            first_head,
            q_norms,
            head,
            group,
            state,
            last,
            tile,
            row,
        )

    def label(far):
        distances = [along_distance(level) for level in range(2, levels + 1)]
        distances += [across_distance(level) for level in range(1, levels + 1)]
        return list(zip(far, distances))

    def mine_rows(h):
        return lambda me: h + lax.rem(me[0], 2) * held if split else h

    def their_rows(h):
        return lambda me: h + (1 - lax.rem(me[0], 2)) * held

    parts = []

    def finish(got, h):
        parts.append((got[0], 0, mine_rows(h)))
        if split:
            parts.append((other_core(got[1]), 0, their_rows(h)))

    for h in range(held):
        own = owns[h] if h == 0 else after(owns[h], along[-1])
        along = [own, next_z(own)]
        if h == 0:
            along[1], q_norms = lax.optimization_barrier((along[1], q_norms))
        else:
            along[1], far = lax.optimization_barrier((along[1], far))
        across = []
        for level in range(1, levels):
            along.append(next_z(along[level]))
            across.append(other_y(along[level]))
            if level == 1 and h == 0 and held > 1:
                near = [(own, along_distance(0)), (along[1], along_distance(1))]
                state = call(near, h, sides, None, False)
                along[2], across[0], state = lax.optimization_barrier(
                    (along[2], across[0], state)
                )
            if level == 1 and h > 0:
                got = [call(label(far), h - 1, (k,), state, True)[0] for k in sides[1:]]
                along[2], across[0], got = lax.optimization_barrier((along[2], across[0], got))
        across.append(other_y(jnp.where(is_y0, own, along[-1])))
        if h > 0:
            got = [call(label(far), h - 1, sides[:1], state, True)[0]] + got
            across[-1], got = lax.optimization_barrier((across[-1], got))
            finish(got, h - 1)
        near = [(own, along_distance(0)), (along[1], along_distance(1))]
        far = along[2:] + across
        if h > 0 and h + 1 < held:
            state = call(near, h, sides, None, False)
    finish(call(near + label(far), held - 1, sides, None, True), held - 1)

    cols = out_weight.shape[1] // tp
    if tp != 2:
        whole = project(me, parts, rows, out_weight, lambda me: 0, cols * tp)
        return lax.psum_scatter(whole, "tp", scatter_dimension=1, tiled=True)
    chunks = 4
    width = cols // chunks
    away, here = [], []
    for c in range(chunks):
        sent = project(
            me, parts, rows, out_weight, lambda me: (1 - me[1]) * cols + c * width, width
        )
        away.append(lax.ppermute(sent, "tp", [(0, 1), (1, 0)]))
    for c in range(chunks):
        here.append(
            project(me, parts, rows, out_weight, lambda me: me[1] * cols + c * width, width)
        )
    return jnp.concatenate(
        [(a.astype(F32) + b.astype(F32)).astype(BF16) for a, b in zip(here, away)], axis=1
    )


def solution(mesh):
    return jax.shard_map(
        local,
        mesh=mesh,
        in_specs=(P("ctx", "tp"), P("ctx", "tp"), P("ctx", "tp"), P("ctx"), P("tp", None)),
        out_specs=P("ctx", "tp"),
        check_vma=False,
    )
```

time: 714 us -> 375 us (0.53); the launches traced: 706 us -> 380 us
  Pallas kernels: 0 us -> 322 us
  waiting for transfers between devices: 237 us -> 37.2 us
  starting transfers between devices: 192 us -> 13.1 us
  matrix products: 165 us -> 0 us
  other arithmetic: 66.8 us -> 2.44 us
  local copies, waits for them, and re-layouts: 26.3 us -> 4.35 us
  between operations: 13.5 us -> 0.54 us
    pallas_call x0 -> x14, Pallas kernels: none -> 322 us  [the longest x4 278 us: attend(): pl.pallas_call(functools.partial(attend_body, head=head, slots=slots, sid...]
    ppermute x16 -> x17, starting transfers between devices: 192 us -> 13.1 us  [the longest x13 8.83 us: permuted(): return lax.ppermute(x, 'ctx', [(i, target(i)) for i in range(ctx)])]
    reduce_scatter x1 -> x0, waiting for transfers between devices: 170 us -> none  [local(): lax.psum_scatter(partial_value.astype(jnp.bfloat16), 'tp', scatter_dimens...]
    dot_general x9 -> x0, matrix products: 165 us -> none  [the longest x4 77.8 us: attend(): jnp.einsum('hgqk,khd->hgqd', weights.astype(jnp.bfloat16), value_heads, p...]
    reduce_sum x4 -> x0, other arithmetic: 60.1 us -> none  [attend(): running_sum = running_sum * rescale + jnp.sum(weights, axis=-1)]
    ppermute x16 -> x17, waiting for transfers between devices: 67.1 us -> 37.2 us  [the longest x13 27.6 us: permuted(): return lax.ppermute(x, 'ctx', [(i, target(i)) for i in range(ctx)])]
    unnamed x6 -> x10, local copies, waits for them, and re-layouts: 14.7 us -> 4.11 us
    while x17 -> x0, local copies, waits for them, and re-layouts: 9.29 us -> none  [the longest x1 8.73 us: local(): lax.fori_loop(1, reach + 1, relay_step, (state, stacked_keys, stacked_val...]
  transfers between devices with their start and end apart: 17 -> 17, of which waited for: 13 -> 8; matrix products, arithmetic and copies ran while one was open for 0% -> 0% of each run, Pallas kernels for 0% -> 46%
where the time goes in v1:
time: 375 us; the launch traced here: 380 us
  Pallas kernels  322 us (86%)
  waiting for transfers between devices  37.2 us (10%)
  starting transfers between devices  13.1 us (3%)
  local copies, waits for them, and re-layouts  4.35 us (1%)
    pallas_call x4, Pallas kernels, attend(): pl.pallas_call(functools.partial(attend_body, head=head, slots=slots, sid...  278 us
    pallas_call x8, Pallas kernels, project(): pl.pallas_call(functools.partial(project_body, blocks=[block for _, _, bl...  38.1 us
    ppermute x13, waiting for transfers between devices, permuted(): return lax.ppermute(x, 'ctx', [(i, target(i)) for i in range(ctx)])  27.6 us
    ppermute x4, waiting for transfers between devices, local(): away.append(lax.ppermute(sent, 'tp', [(0, 1), (1, 0)]))  9.57 us
    ppermute x13, starting transfers between devices, permuted(): return lax.ppermute(x, 'ctx', [(i, target(i)) for i in range(ctx)])  8.83 us
  transfers between devices with their start and end apart: 17, of which 8 were waited for; matrix products, arithmetic and copies ran while one was open for 0% of the time, Pallas kernels for 46%

profile of v1, /device:TPU:24, one launch (start us, length us, event | category | flops | bytes accessed | tf_op | source)
XLA Modules:
  0.0 379.7 jit_solution(11880633875955318108)
XLA Ops:
  0.1 1.0 copy-done
  1.1 1.0 copy-done.1
  2.2 1.1 pack.1
  3.4 1.9 collective-permute-done
  6.1 6.9 %collective-permute-done.2.refs_1_.refs_7_.refs_10_ = bf16[512,4096]{1,0:T(8,128)(2,1)} collective-permute-done((bf16[512,4096]{1,0:T(8,128)(2,1)}, bf16[512,4096]{1,0:T(8,128)(2,1)}, u32[]{:S(2)}, u32[]{:S(2)}) %collective-permute-start.2) | collective-permute-done | bytes 4194336 | tf_op jit(solution)/shard_map/ppermute | solution.py:367
  12.9 4.5 %norms.1.refs_8_.refs_11_ = f32[4]{0:T(128)S(1)} custom-call(s32[2]{0:T(128)S(1)} %pad_add_fusion.me_ref, bf16[512,4096]{1,0:T(8,128)(2,1)} %refs_9_.1, bf16[512,4096]{1,0:T(8,128)(2,1)} %collective-permute-done.2.refs_1_.refs_7_.refs_10_), custom_call_target="tpu_custom_call" | custom-call | tf_op jit(solution)/shard_map/norms/pallas_call | solution.py:70
  17.4 2.3 collective-permute-done.1
  19.8 2.1 collective-permute-start.3
  22.0 1.5 collective-permute-start.4
  23.5 56.4 %attend.4 = (f32[2,8,128,512]{3,2,1,0:T(8,128)S(1)}, f32[2,8,16,512]{3,2,1,0:T(8,128)S(1)}, s32[2]{0:T(128)S(1)}) custom-call(s32[2]{0:T(128)S(1)} %pad_add_fusion.me_ref, s32[512]{0:T(512)S(1)} %copy-done.2, s32[512]{0:T(512)S(1)} %collective-permute-done.5.refs_1_, bf16[2,2,512,128]{3,2,1,0:T(8,128)(2,1)S(1)} %copy.6.refs_2_, ...), custom_call_target="tpu_custom_call" | custom-call | flops 12884901888 | bytes 8388608 | tf_op jit(solution)/shard_map/attend/pallas_call | solution.py:277
  79.9 2.0 copy-done.3
  82.1 12.8 %collective-permute-done.7 = bf16[2,2,512,128]{3,2,0,1:T(8,128)(2,1)S(1)} collective-permute-done((bf16[2,2,512,128]{3,2,0,1:T(8,128)(2,1)S(1)}, bf16[2,2,512,128]{3,2,0,1:T(8,128)(2,1)S(1)}, u32[]{:S(2)}, u32[]{:S(2)}) %collective-permute-start.7) | collective-permute-done | bytes 524320 | tf_op jit(solution)/shard_map/ppermute | solution.py:367
  95.0 2.1 collective-permute-start.8
  97.1 1.7 collective-permute-start.9
  98.9 40.8 %attend.5 = bf16[512,1024]{1,0:T(8,128)(2,1)S(1)} custom-call(s32[2]{0:T(128)S(1)} %pad_add_fusion.me_ref, s32[512]{0:T(512)S(1)} %copy-done.2, s32[512]{0:T(512)S(1)} %collective-permute-done.5.refs_1_, bf16[2,2,512,128]{3,2,1,0:T(8,128)(2,1)S(1)} %copy.8.refs_2_, bf16[2,2,512,128]{3,2,1,0:T(8,128)(2,1)S(1)} %copy.9.refs_3_, ...), custom_call_target="tpu_custom_call" | custom-call | flops 9663676416 | bytes 8388608 | tf_op jit(solution)/shard_map/attend/pallas_call | solution.py:277
  139.9 40.5 %attend.6.refs_0_ = bf16[512,1024]{1,0:T(8,128)(2,1)S(1)} custom-call(s32[2]{0:T(128)S(1)} %pad_add_fusion.me_ref, s32[512]{0:T(512)S(1)} %copy-done.2, s32[512]{0:T(512)S(1)} %collective-permute-done.5.refs_1_, bf16[2,2,512,128]{3,2,1,0:T(8,128)(2,1)S(1)} %copy.8.refs_2_, bf16[2,2,512,128]{3,2,1,0:T(8,128)(2,1)S(1)} %copy.9.refs_3_, ...), custom_call_target="tpu_custom_call" | custom-call | flops 9663676416 | bytes 8388608 | tf_op jit(solution)/shard_map/attend/pallas_call | solution.py:277
  180.4 140.6 %attend.7 = (bf16[512,1024]{1,0:T(8,128)(2,1)S(1)}, bf16[512,1024]{1,0:T(8,128)(2,1)S(1)}) custom-call(s32[2]{0:T(128)S(1)} %pad_add_fusion.me_ref, s32[512]{0:T(512)S(1)} %copy-done.2, s32[512]{0:T(512)S(1)} %collective-permute-done.5.refs_1_, bf16[2,2,512,128]{3,2,1,0:T(8,128)(2,1)S(1)} %pad_maximum_fusion.1.refs_2_, ...), custom_call_target="tpu_custom_call" | custom-call | flops 32212254720 | bytes 8388608 | tf_op jit(solution)/shard_map/attend/pallas_call | solution.py:277
  321.6 2.1 collective-permute-done.12.refs_3_
  323.8 1.5 collective-permute-done.11.refs_1_
  325.3 4.7 %project.9 = bf16[512,512]{1,0:T(8,128)(2,1)S(1)} custom-call(s32[2]{0:T(128)S(1)} %pad_add_fusion.me_ref, bf16[512,1024]{1,0:T(8,128)(2,1)S(1)} %attend.6.refs_0_, bf16[512,1024]{1,0:T(8,128)(2,1)S(1)} %collective-permute-done.11.refs_1_, bf16[512,1024]{1,0:T(8,128)(2,1)S(1)} %get-tuple-element.57.refs_2_, ...), custom_call_target="tpu_custom_call" | custom-call | flops 2147483648 | bytes 4194304 | tf_op jit(solution)/shard_map/project/pallas_call | solution.py:334
  330.0 1.6 collective-permute-start.13
  331.6 4.7 %project.11 = bf16[512,512]{1,0:T(8,128)(2,1)S(1)} custom-call(s32[2]{0:T(128)S(1)} %pad_add_fusion.me_ref, bf16[512,1024]{1,0:T(8,128)(2,1)S(1)} %attend.6.refs_0_, bf16[512,1024]{1,0:T(8,128)(2,1)S(1)} %collective-permute-done.11.refs_1_, bf16[512,1024]{1,0:T(8,128)(2,1)S(1)} %get-tuple-element.57.refs_2_, ...), custom_call_target="tpu_custom_call" | custom-call | flops 2147483648 | bytes 4194304 | tf_op jit(solution)/shard_map/project/pallas_call | solution.py:334
  336.3 0.6 collective-permute-start.14
  336.9 4.7 %project.13 = bf16[512,512]{1,0:T(8,128)(2,1)S(1)} custom-call(s32[2]{0:T(128)S(1)} %pad_add_fusion.me_ref, bf16[512,1024]{1,0:T(8,128)(2,1)S(1)} %attend.6.refs_0_, bf16[512,1024]{1,0:T(8,128)(2,1)S(1)} %collective-permute-done.11.refs_1_, bf16[512,1024]{1,0:T(8,128)(2,1)S(1)} %get-tuple-element.57.refs_2_, ...), custom_call_target="tpu_custom_call" | custom-call | flops 2147483648 | bytes 4194304 | tf_op jit(solution)/shard_map/project/pallas_call | solution.py:334
  341.7 1.6 collective-permute-start.15
  343.2 4.9 %project.15 = bf16[512,512]{1,0:T(8,128)(2,1)S(1)} custom-call(s32[2]{0:T(128)S(1)} %pad_add_fusion.me_ref, bf16[512,1024]{1,0:T(8,128)(2,1)S(1)} %attend.6.refs_0_, bf16[512,1024]{1,0:T(8,128)(2,1)S(1)} %collective-permute-done.11.refs_1_, bf16[512,1024]{1,0:T(8,128)(2,1)S(1)} %get-tuple-element.57.refs_2_, ...), custom_call_target="tpu_custom_call" | custom-call | flops 2147483648 | bytes 4194304 | tf_op jit(solution)/shard_map/project/pallas_call | solution.py:334
  348.8 4.7 %project.8 = bf16[512,512]{1,0:T(8,128)(2,1)S(1)} custom-call(s32[2]{0:T(128)S(1)} %pad_add_fusion.me_ref, bf16[512,1024]{1,0:T(8,128)(2,1)S(1)} %attend.6.refs_0_, bf16[512,1024]{1,0:T(8,128)(2,1)S(1)} %collective-permute-done.11.refs_1_, bf16[512,1024]{1,0:T(8,128)(2,1)S(1)} %get-tuple-element.57.refs_2_, ...), custom_call_target="tpu_custom_call" | custom-call | flops 2147483648 | bytes 4194304 | tf_op jit(solution)/shard_map/project/pallas_call | solution.py:334
  353.5 4.7 %project.10 = bf16[512,512]{1,0:T(8,128)(2,1)S(1)} custom-call(s32[2]{0:T(128)S(1)} %pad_add_fusion.me_ref, bf16[512,1024]{1,0:T(8,128)(2,1)S(1)} %attend.6.refs_0_, bf16[512,1024]{1,0:T(8,128)(2,1)S(1)} %collective-permute-done.11.refs_1_, bf16[512,1024]{1,0:T(8,128)(2,1)S(1)} %get-tuple-element.57.refs_2_, ...), custom_call_target="tpu_custom_call" | custom-call | flops 2147483648 | bytes 4194304 | tf_op jit(solution)/shard_map/project/pallas_call | solution.py:334
  358.2 4.7 %project.12 = bf16[512,512]{1,0:T(8,128)(2,1)S(1)} custom-call(s32[2]{0:T(128)S(1)} %pad_add_fusion.me_ref, bf16[512,1024]{1,0:T(8,128)(2,1)S(1)} %attend.6.refs_0_, bf16[512,1024]{1,0:T(8,128)(2,1)S(1)} %collective-permute-done.11.refs_1_, bf16[512,1024]{1,0:T(8,128)(2,1)S(1)} %get-tuple-element.57.refs_2_, ...), custom_call_target="tpu_custom_call" | custom-call | flops 2147483648 | bytes 4194304 | tf_op jit(solution)/shard_map/project/pallas_call | solution.py:334
  363.0 4.7 %project.14 = bf16[512,512]{1,0:T(8,128)(2,1)S(1)} custom-call(s32[2]{0:T(128)S(1)} %pad_add_fusion.me_ref, bf16[512,1024]{1,0:T(8,128)(2,1)S(1)} %attend.6.refs_0_, bf16[512,1024]{1,0:T(8,128)(2,1)S(1)} %collective-permute-done.11.refs_1_, bf16[512,1024]{1,0:T(8,128)(2,1)S(1)} %get-tuple-element.57.refs_2_, ...), custom_call_target="tpu_custom_call" | custom-call | flops 2147483648 | bytes 4194304 | tf_op jit(solution)/shard_map/project/pallas_call | solution.py:334
  368.2 9.6 %collective-permute-done.16 = bf16[512,512]{1,0:T(8,128)(2,1)S(1)} collective-permute-done((bf16[512,512]{1,0:T(8,128)(2,1)S(1)}, bf16[512,512]{1,0:T(8,128)(2,1)S(1)}, u32[]{:S(2)}, u32[]{:S(2)}) %collective-permute-start.16) | collective-permute-done | bytes 524320 | tf_op jit(solution)/shard_map/ppermute | solution.py:485
  377.9 1.6 pad_maximum_fusion
  (43 shorter events, 3.2 us)
Async XLA Ops:
  0.0 5.6 %copy-start.2 = (s32[512]{0:T(512)S(1)}, s32[512]{0:T(512)}, u32[]{:S(2)}) copy-start(s32[512]{0:T(512)} %refs_0_.11) | copy-start | bytes 6148
  0.1 1.0 copy-start
  1.1 1.0 copy-start.1
  3.3 2.0 collective-permute-start
  5.4 7.6 %collective-permute-start.2 = (bf16[512,4096]{1,0:T(8,128)(2,1)}, bf16[512,4096]{1,0:T(8,128)(2,1)}, u32[]{:S(2)}, u32[]{:S(2)}) collective-permute-start(bf16[512,4096]{1,0:T(8,128)(2,1)} %refs_9_.1), channel_id=1, source_target_pairs={{0,2},{2,0},{4,6},{6,4},{8,10},{10,8},{12,14},{14,12},{16,18},{18,... | collective-permute-start | bytes 12582920 | tf_op jit(solution)/shard_map/ppermute | solution.py:367
  5.6 14.2 %collective-permute-start.1 = (bf16[2,2,512,128]{3,2,0,1:T(8,128)(2,1)S(1)}, bf16[2,2,512,128]{3,2,0,1:T(8,128)(2,1)S(1)}, u32[]{:S(2)}, u32[]{:S(2)}) collective-permute-start(bf16[2,2,512,128]{3,2,0,1:T(8,128)(2,1)S(1)} %pad_maximum_fusion.2), channel_id=1, source_target_pairs={{0,8},{2,10},{4,12},{6,14},{8,16},{10,18},{12,20},{14,22},{16,24},... | collective-permute-start | bytes 1572872 | tf_op jit(solution)/shard_map/ppermute | solution.py:367
  5.6 17.9 %collective-permute-start.5 = (s32[512]{0:T(512)S(1)}, s32[512]{0:T(512)S(1)}, u32[]{:S(2)}, u32[]{:S(2)}) collective-permute-start(s32[512]{0:T(512)S(1)} %copy-done.2), channel_id=1, source_target_pairs={{0,2},{2,0},{4,6},{6,4},{8,10},{10,8},{12,14},{14,12},{16,18},{18,... | collective-permute-start | bytes 6152 | tf_op jit(solution)/shard_map/ppermute | solution.py:367
  19.8 62.1 %collective-permute-start.3 = (bf16[2,2,512,128]{3,2,0,1:T(8,128)(2,1)S(1)}, bf16[2,2,512,128]{3,2,0,1:T(8,128)(2,1)S(1)}, u32[]{:S(2)}, u32[]{:S(2)}) collective-permute-start(bf16[2,2,512,128]{3,2,0,1:T(8,128)(2,1)S(1)} %collective-permute-done.1), channel_id=1, source_target_pairs={{0,8},{2,10},{4,12},{6,14},{8,16},{10,18},{12,20},{14,22},{16,24},... | collective-permute-start | bytes 1572872 | tf_op jit(solution)/shard_map/ppermute | solution.py:367
  22.0 59.9 %collective-permute-start.4 = (bf16[2,2,512,128]{3,2,0,1:T(8,128)(2,1)S(1)}, bf16[2,2,512,128]{3,2,0,1:T(8,128)(2,1)S(1)}, u32[]{:S(2)}, u32[]{:S(2)}) collective-permute-start(bf16[2,2,512,128]{3,2,0,1:T(8,128)(2,1)S(1)} %collective-permute-done.1), channel_id=1, source_target_pairs={{0,4},{2,6},{4,0},{6,2},{8,12},{10,14},{12,8},{14,10},{16,20},{18,... | collective-permute-start | bytes 1572872 | tf_op jit(solution)/shard_map/ppermute | solution.py:367
  79.9 2.0 copy-start.3
  81.9 17.0 %copy-start.4 = (f32[2,8,128,512]{3,2,1,0:T(8,128)S(1)}, f32[2,8,128,512]{3,2,1,0:T(8,128)}, u32[]{:S(2)}) copy-start(f32[2,8,128,512]{3,2,1,0:T(8,128)} %copy-done.3) | copy-start | bytes 12582916
  82.0 13.0 %collective-permute-start.7 = (bf16[2,2,512,128]{3,2,0,1:T(8,128)(2,1)S(1)}, bf16[2,2,512,128]{3,2,0,1:T(8,128)(2,1)S(1)}, u32[]{:S(2)}, u32[]{:S(2)}) collective-permute-start(bf16[2,2,512,128]{3,2,0,1:T(8,128)(2,1)S(1)} %broadcast_select_fusion.1), channel_id=1, source_target_pairs={{0,4},{2,6},{4,0},{6,2},{8,12},{10,14},{12,8},{14,10},{16,20},{18,... | collective-permute-start | bytes 1572872 | tf_op jit(solution)/shard_map/ppermute | solution.py:367
  82.1 13.0 %collective-permute-start.6 = (bf16[2,2,512,128]{3,2,1,0:T(8,128)(2,1)S(1)}, bf16[2,2,512,128]{3,2,1,0:T(8,128)(2,1)S(1)}, u32[]{:S(2)}, u32[]{:S(2)}) collective-permute-start(bf16[2,2,512,128]{3,2,1,0:T(8,128)(2,1)S(1)} %pad_maximum_fusion.1.refs_2_), channel_id=1, source_target_pairs={{0,8},{2,10},{4,12},{6,14},{8,16},{10,18},{12,20},{14,22},{16,24},... | collective-permute-start | bytes 1572872 | tf_op jit(solution)/shard_map/ppermute | solution.py:367
  95.0 44.7 %collective-permute-start.8 = (bf16[2,2,512,128]{3,2,1,0:T(8,128)(2,1)S(1)}, bf16[2,2,512,128]{3,2,1,0:T(8,128)(2,1)S(1)}, u32[]{:S(2)}, u32[]{:S(2)}) collective-permute-start(bf16[2,2,512,128]{3,2,1,0:T(8,128)(2,1)S(1)} %collective-permute-done.6.refs_3_), channel_id=1, source_target_pairs={{0,8},{2,10},{4,12},{6,14},{8,16},{10,18},{12,20},{14,22},{16,24},... | collective-permute-start | bytes 1572872 | tf_op jit(solution)/shard_map/ppermute | solution.py:367
  97.1 42.6 %collective-permute-start.9 = (bf16[2,2,512,128]{3,2,1,0:T(8,128)(2,1)S(1)}, bf16[2,2,512,128]{3,2,1,0:T(8,128)(2,1)S(1)}, u32[]{:S(2)}, u32[]{:S(2)}) collective-permute-start(bf16[2,2,512,128]{3,2,1,0:T(8,128)(2,1)S(1)} %collective-permute-done.6.refs_3_), channel_id=1, source_target_pairs={{0,4},{2,6},{4,0},{6,2},{8,12},{10,14},{12,8},{14,10},{16,20},{18,... | collective-permute-start | bytes 1572872 | tf_op jit(solution)/shard_map/ppermute | solution.py:367
  139.8 40.6 %collective-permute-start.10 = (bf16[2,2,512,128]{3,2,1,0:T(8,128)(2,1)S(1)}, bf16[2,2,512,128]{3,2,1,0:T(8,128)(2,1)S(1)}, u32[]{:S(2)}, u32[]{:S(2)}) collective-permute-start(bf16[2,2,512,128]{3,2,1,0:T(8,128)(2,1)S(1)} %broadcast_select_fusion), channel_id=1, source_target_pairs={{0,4},{2,6},{4,0},{6,2},{8,12},{10,14},{12,8},{14,10},{16,20},{18,... | collective-permute-start | bytes 1572872 | tf_op jit(solution)/shard_map/ppermute | solution.py:367
  321.1 2.7 collective-permute-start.12
  321.1 4.1 %collective-permute-start.11 = (bf16[512,1024]{1,0:T(8,128)(2,1)S(1)}, bf16[512,1024]{1,0:T(8,128)(2,1)S(1)}, u32[]{:S(2)}, u32[]{:S(2)}) collective-permute-start(bf16[512,1024]{1,0:T(8,128)(2,1)S(1)} %attend.5), channel_id=1, source_target_pairs={{0,2},{2,0},{4,6},{6,4},{8,10},{10,8},{12,14},{14,12},{16,18},{18,... | collective-permute-start | bytes 3145736 | tf_op jit(solution)/shard_map/ppermute | solution.py:367
  330.0 37.7 %collective-permute-start.13 = (bf16[512,512]{1,0:T(8,128)(2,1)S(1)}, bf16[512,512]{1,0:T(8,128)(2,1)S(1)}, u32[]{:S(2)}, u32[]{:S(2)}) collective-permute-start(bf16[512,512]{1,0:T(8,128)(2,1)S(1)} %project.9), channel_id=1, source_target_pairs={{0,1},{1,0},{2,3},{3,2},{4,5},{5,4},{6,7},{7,6},{8,9},{9,8},{10,11... | collective-permute-start | bytes 1572872 | tf_op jit(solution)/shard_map/ppermute | solution.py:485
  336.3 31.6 %collective-permute-start.14 = (bf16[512,512]{1,0:T(8,128)(2,1)S(1)}, bf16[512,512]{1,0:T(8,128)(2,1)S(1)}, u32[]{:S(2)}, u32[]{:S(2)}) collective-permute-start(bf16[512,512]{1,0:T(8,128)(2,1)S(1)} %project.11), channel_id=1, source_target_pairs={{0,1},{1,0},{2,3},{3,2},{4,5},{5,4},{6,7},{7,6},{8,9},{9,8},{10,11... | collective-permute-start | bytes 1572872 | tf_op jit(solution)/shard_map/ppermute | solution.py:485
  341.7 26.4 %collective-permute-start.15 = (bf16[512,512]{1,0:T(8,128)(2,1)S(1)}, bf16[512,512]{1,0:T(8,128)(2,1)S(1)}, u32[]{:S(2)}, u32[]{:S(2)}) collective-permute-start(bf16[512,512]{1,0:T(8,128)(2,1)S(1)} %project.13), channel_id=1, source_target_pairs={{0,1},{1,0},{2,3},{3,2},{4,5},{5,4},{6,7},{7,6},{8,9},{9,8},{10,11... | collective-permute-start | bytes 1572872 | tf_op jit(solution)/shard_map/ppermute | solution.py:485
  348.2 29.6 %collective-permute-start.16 = (bf16[512,512]{1,0:T(8,128)(2,1)S(1)}, bf16[512,512]{1,0:T(8,128)(2,1)S(1)}, u32[]{:S(2)}, u32[]{:S(2)}) collective-permute-start(bf16[512,512]{1,0:T(8,128)(2,1)S(1)} %project.15), channel_id=1, source_target_pairs={{0,1},{1,0},{2,3},{3,2},{4,5},{5,4},{6,7},{7,6},{8,9},{9,8},{10,11... | collective-permute-start | bytes 1572872 | tf_op jit(solution)/shard_map/ppermute | solution.py:485
